TPU v7x, 256 devices: a whole 4x4x8 slice. The times are simulated.
256 devices in a mesh: dp: 32 (over z, x), tensor: 8 (over y, core).
Axes of the slice: x: 4, y: 4, z: 8, core: 2. Of those that a mesh axis runs over, the one named last changes fastest.
Arguments:
- activations: bfloat16 [28672, 4096], P('dp', 'tensor'), may hold values from -6 to 6
- out_grads: bfloat16 [28672, 4096], P('dp', 'tensor'), may hold values from -6 to 6
- gate_act: bfloat16 [28672, 14336], P('dp', 'tensor'), may hold values from -6 to 6
- w_down: bfloat16 [14336, 4096], P('tensor', 'dp'), may hold values from -0.09375 to 0.09375
- proj_in: bfloat16 [4096, 64], P('tensor'), may hold values from -0.09375 to 0.09375
- proj_out: bfloat16 [14336, 64], P('tensor'), may hold values from -0.046875 to 0.046875
- lengths: int32 [32, 8], P('dp'), may hold values from 1 to 448, 896 in all within a row
- assign: int32 [256], replicated, may hold values from 0 to 255, each once
Outputs:
- loggrads: float32 [256, 64, 64], P('dp', 'tensor')
Inputs may be any that keep to these rules, and one draw needn't show every extreme that they name: `lengths`: each row gives the token counts of the 8 sequences packed into one data group's 896 rows and sums to 896. `assign`: a permutation of the sequence numbers.
All inputs are finite; a program needn't handle non-finite values.
Results may differ from a plain program's by a relative error of at most 0.013.
Values may be sent and summed in bfloat16 or wider, within the bound.
No kernel may reach another device: no remote copies, remote signals or barrier semaphores. Data moves between devices by JAX's collectives and lax.ppermute only.
A program may use at most 128 MiB of HBM per device.

v0:
```python
import jax
import jax.numpy as jnp
from jax import lax
from jax.sharding import PartitionSpec as P


def member_of(seq_lengths, tok_rows):
    slots = seq_lengths.shape[0]
    before = lax.iota(jnp.int32, slots)[None, :] < lax.iota(jnp.int32, slots)[:, None]
    starts = jnp.sum(jnp.where(before, seq_lengths[None, :], 0), axis=1)
    ends = starts + seq_lengths
    positions = lax.iota(jnp.int32, tok_rows)
    inside = (positions[None, :] >= starts[:, None]) & (positions[None, :] < ends[:, None])
    return jnp.where(inside, 1.0 / seq_lengths[:, None].astype(jnp.float32), 0.0)


def place(result, assign):
    slots, values = result.shape
    groups = lax.axis_size("dp")
    mine = lax.dynamic_slice_in_dim(assign, lax.axis_index("dp") * slots, slots, 0)
    placing = (mine[None, :] == lax.iota(jnp.int32, slots * groups)[:, None]).astype(jnp.bfloat16)
    spread = jnp.dot(placing, result, preferred_element_type=jnp.float32).astype(jnp.bfloat16)
    got = lax.all_to_all(spread, "dp", split_axis=0, concat_axis=0, tiled=True)
    return jnp.sum(got.reshape(groups, slots, values).astype(jnp.float32), axis=0)


def shards(activations, out_grads, gate_act, w_down, proj_in, proj_out, lengths, assign):
    tok_rows = activations.shape[0]
    rank_all = proj_in.shape[1]
    shard_count = lax.axis_size("tensor")
    slots = lengths.shape[1]
    cols = rank_all // shard_count
    in_part = jnp.dot(activations, proj_in, preferred_element_type=jnp.float32)
    in_high = in_part.astype(jnp.bfloat16)
    in_low = (in_part - in_high.astype(jnp.float32)).astype(jnp.bfloat16)
    full_grads = lax.all_gather(out_grads, "tensor", axis=1, tiled=True)
    in_all = lax.all_gather(jnp.concatenate([in_high, in_low], axis=1), "tensor", axis=0)
    in_all = jnp.sum(in_all.astype(jnp.float32), axis=0)
    in_sum = in_all[:, :rank_all] + in_all[:, rank_all:]
    weighted = member_of(lengths[0], tok_rows)[:, :, None] * in_sum[None, :, :]
    hidden_grad = lax.dot_general(
        full_grads,
        lax.all_gather(w_down, "dp", axis=1, tiled=True),
        (((1,), (1,)), ((), ())),
        preferred_element_type=jnp.float32,
    )
    up_grad = (hidden_grad * gate_act.astype(jnp.float32)).astype(jnp.bfloat16)
    out_part = jnp.dot(up_grad, proj_out, preferred_element_type=jnp.float32)
    part = jnp.einsum("ctp,tq->cpq", weighted, out_part, precision=lax.Precision.HIGHEST)
    part = part.reshape(slots, shard_count, cols * rank_all).transpose(1, 0, 2)
    result = jnp.sum(
        lax.all_to_all(part, "tensor", split_axis=0, concat_axis=0, tiled=True), axis=0
    )
    return place(result.astype(jnp.bfloat16), assign).reshape(slots, cols, rank_all)


def solution(mesh):
    in_specs = (
        P("dp", "tensor"),
        P("dp", "tensor"),
        P("dp", "tensor"),
        P("tensor", "dp"),
        P("tensor", None),
        P("tensor", None),
        P("dp", None),
        P(),
    )
    out_specs = P("dp", "tensor", None)
    return jax.shard_map(shards, mesh=mesh, in_specs=in_specs, out_specs=out_specs, check_vma=False)
```

profile of v0, /device:TPU:32, one launch (start us, length us, event | category | flops | bytes accessed | tf_op | source)
XLA Modules:
  0.0 291.1 jit_solution(1241002359419916471)
XLA Ops:
  6.5 0.0 copy-start
  6.5 0.0 all-gather.9.cloned.1.call-start
  6.5 1.2 copy-done
  7.7 1.3 subtract_convert_fusion
  9.0 0.7 pad_maximum_fusion
  9.7 0.0 all-gather.9.cloned.1.call-update
  9.7 0.0 all-gather.5.cloned.1.call-start
  9.8 0.7 all-gather.5.cloned.1.call-update
  10.5 0.0 all-gather.7.cloned.1.call-start
  10.5 0.7 all-gather.7.cloned.1.call-update
  11.2 0.8 select_reduce_fusion
  12.0 0.7 convert_divide_fusion
  12.7 0.7 bitcast_add_fusion
  13.3 0.1 fusion.9
  13.4 26.7 %all-gather.9.cloned.1.call-done = bf16[7168,128]{0,1:T(8,128)(2,1)} async-done(((bf16[896,128]{0,1:T(8,128)(2,1)}), bf16[7168,128]{0,1:T(8,128)(2,1)}) %all-gather.9.cloned.1.call-update) | async-done | bytes 1835024 | tf_op jit(solution)/shard_map/all_gather | solution.py:37
  40.1 1.9 convert_element_type.46
  42.0 0.0 copy-start.1
  42.0 0.6 copy.11
  42.7 0.9 bitcast_reduce_fusion
  43.6 0.0 copy-start.2
  43.6 46.3 %all-gather.5.cloned.1.call-done = bf16[896,4096]{1,0:T(8,128)(2,1)} async-done(((bf16[896,512]{1,0:T(8,128)(2,1)}), bf16[896,4096]{1,0:T(8,128)(2,1)}) %all-gather.5.cloned.1.call-update) | async-done | bytes 7340048 | tf_op jit(solution)/shard_map/all_gather | solution.py:36
  89.8 141.1 %all-gather.7.cloned.1.call-done = bf16[1792,4096]{1,0:T(8,128)(2,1)} async-done(((bf16[1792,128]{1,0:T(8,128)(2,1)}), bf16[1792,4096]{1,0:T(8,128)(2,1)}) %all-gather.7.cloned.1.call-update) | async-done | bytes 14680080 | tf_op jit(solution)/shard_map/all_gather | solution.py:43
  230.9 22.0 %fusion.4 = f32[896,64,1]{0,1,2:T(8,128)S(1)} fusion(bf16[1792,64]{0,1:T(8,128)(2,1)S(1)} %copy-done.1, bf16[896,1792]{1,0:T(8,128)(2,1)} %param.10, bf16[896,4096]{1,0:T(8,128)(2,1)} %all-gather.5.cloned.1.call-done, bf16[1792,4096]{1,0:T(8,128)(2,1)} %all-gather.7.cloned.1.call-done), kind=kOutput, calls=%fused_computation.7 | convolution fusion | flops 13363675136 | bytes 25690112 | tf_op jit(solution)/shard_map/dot_general | solution.py:48
  253.0 1.7 fusion.1
  254.6 0.1 reshape.85
  254.8 0.7 copy.13
  255.5 4.3 %all-to-all-start = ((f32[8,8,512]{2,1,0:T(8,128)}), f32[8,8,512]{2,1,0:T(8,128)S(1)}, u32[]{:S(2)}, u32[]{:S(2)}) async-start(f32[8,8,512]{2,1,0:T(8,128)} %bitcast.21), calls=%async_computation | async-start | bytes 262144 | tf_op jit(solution)/shard_map/all_to_all | solution.py:52
  259.8 0.1 dynamic_slice.3
  259.8 6.1 %all-to-all-done = f32[8,8,512]{2,1,0:T(8,128)S(1)} async-done(((f32[8,8,512]{2,1,0:T(8,128)}), f32[8,8,512]{2,1,0:T(8,128)S(1)}, u32[]{:S(2)}, u32[]{:S(2)}) %all-to-all-start) | async-done | bytes 131104 | tf_op jit(solution)/shard_map/all_to_all | solution.py:52
  265.9 0.2 fusion.3
  266.1 17.7 %all_to_all.14 = bf16[32,8,512]{2,1,0:T(8,128)(2,1)S(1)} all-to-all(bf16[32,8,512]{2,1,0:T(8,128)(2,1)S(1)} %fusion.3), channel_id=1, replica_groups=mesh['dp'=32,'tensor'=8] {'dp'}, dimensions={0} | all-to-all | bytes 524288 | tf_op jit(solution)/shard_map/all_to_all | solution.py:23
  283.9 0.7 reshape.86
  (5 shorter events, 0.1 us)
Async XLA Ops:
  6.5 1.2 copy-start
  6.5 33.6 %all-gather.9.cloned.1.call-start = ((), (), s32[]{:S(2)}) async-start(), calls=%async_computation.4 | async-start | bytes 2064384 | tf_op jit(solution)/shard_map/all_gather | solution.py:37
  9.7 80.1 %all-gather.5.cloned.1.call-start = ((), (), s32[]{:S(2)}) async-start(), calls=%async_computation.2 | async-start | bytes 8257536 | tf_op jit(solution)/shard_map/all_gather | solution.py:36
  10.5 220.4 %all-gather.7.cloned.1.call-start = ((), (), s32[]{:S(2)}) async-start(), calls=%async_computation.3 | async-start | bytes 15138816 | tf_op jit(solution)/shard_map/all_gather | solution.py:43
  42.0 188.9 %copy-start.1 = (bf16[1792,64]{0,1:T(8,128)(2,1)S(1)}, bf16[1792,64]{0,1:T(8,128)(2,1)}, u32[]{:S(2)}) copy-start(bf16[1792,64]{0,1:T(8,128)(2,1)} %param.13) | copy-start | bytes 688132
  43.6 216.2 %copy-start.2 = (s32[256]{0:T(256)S(1)}, s32[256]{0:T(256)}, u32[]{:S(2)}) copy-start(s32[256]{0:T(256)} %param.15) | copy-start | bytes 3076
  255.5 10.4 %all-to-all-start = ((f32[8,8,512]{2,1,0:T(8,128)}), f32[8,8,512]{2,1,0:T(8,128)S(1)}, u32[]{:S(2)}, u32[]{:S(2)}) async-start(f32[8,8,512]{2,1,0:T(8,128)} %bitcast.21), calls=%async_computation | async-start | bytes 262144 | tf_op jit(solution)/shard_map/all_to_all | solution.py:52
Sparse Core Ops, SparseCore 0:
  9.9 30.2 all-gather.8
  42.0 47.8 all-gather.4
  92.3 138.5 all-gather.6
where the time goes:
time: 291 us
  waiting for transfers between devices  222 us (76%)
  matrix products  25.2 us (9%)
  blocking collectives  17.7 us (6%)
  between operations  13.2 us (5%)
  other arithmetic  5.72 us (2%)
  starting transfers between devices  4.37 us (2%)
  local copies, waits for them, and re-layouts  3.43 us (1%)
    all_gather x1, waiting for transfers between devices, shards(): lax.all_gather(w_down, 'dp', axis=1, tiled=True)  141 us
    all_gather x1, waiting for transfers between devices, shards(): full_grads = lax.all_gather(out_grads, 'tensor', axis=1, tiled=True)  46.3 us
    all_gather x1, waiting for transfers between devices, shards(): lax.all_gather(jnp.concatenate([in_high, in_low], axis=1), 'tensor', axis=0)  26.7 us
    dot_general x1, matrix products, shards(): out_part = jnp.dot(up_grad, proj_out, preferred_element_type=jnp.float32)  22 us
    all_to_all x1, blocking collectives, place(): got = lax.all_to_all(spread, 'dp', split_axis=0, concat_axis=0, tiled=True)  17.7 us
    all_to_all x1, waiting for transfers between devices, shards(): lax.all_to_all(part, 'tensor', split_axis=0, concat_axis=0, tiled=True)  6.05 us
  transfers between devices with their start and end apart: 4, of which 4 were waited for; matrix products, arithmetic and copies ran while one was open for 2% of the time, Pallas kernels for 0%

commit v1 on v0

--- a/solution.py
+++ b/solution.py
@@ -33,7 +33,9 @@
     in_part = jnp.dot(activations, proj_in, preferred_element_type=jnp.float32)
     in_high = in_part.astype(jnp.bfloat16)
     in_low = (in_part - in_high.astype(jnp.float32)).astype(jnp.bfloat16)
-    full_grads = lax.all_gather(out_grads, "tensor", axis=1, tiled=True)
+    full_grads = jnp.concatenate(
+        lax.all_to_all(jnp.stack([out_grads] * lax.axis_size("tensor")), "tensor", 0, 0), axis=1
+    )
     in_all = lax.all_gather(jnp.concatenate([in_high, in_low], axis=1), "tensor", axis=0)
     in_all = jnp.sum(in_all.astype(jnp.float32), axis=0)
     in_sum = in_all[:, :rank_all] + in_all[:, rank_all:]

time: 291 us -> 253 us (0.87)
  waiting for transfers between devices: 222 us -> 174 us
  local copies, waits for them, and re-layouts: 3.43 us -> 8.88 us
  starting transfers between devices: 4.37 us -> 9.31 us
    all_gather x1, waiting for transfers between devices: 141 us -> 80.2 us  [shards(): lax.all_gather(w_down, 'dp', axis=1, tiled=True)]
    all_to_all x0 -> x1, waiting for transfers between devices: none -> 55.9 us  [shards(): lax.all_to_all(jnp.stack([out_grads] * lax.axis_size('tensor')), 'tensor'...]
    all_gather x1 -> x0, waiting for transfers between devices: 46.3 us -> none  [shards(): full_grads = lax.all_gather(out_grads, 'tensor', axis=1, tiled=True)]
    all_to_all x0 -> x1, starting transfers between devices: none -> 4.97 us  [shards(): lax.all_to_all(jnp.stack([out_grads] * lax.axis_size('tensor')), 'tensor'...]
    all_gather x1, waiting for transfers between devices: 26.7 us -> 31.2 us  [shards(): lax.all_gather(jnp.concatenate([in_high, in_low], axis=1), 'tensor', axis=0)]
    another operation x0 -> x1, local copies, waits for them, and re-layouts: none -> 3.91 us  [shards(): jnp.stack([out_grads] * lax.axis_size('tensor'))]
  transfers between devices with their start and end apart: 4 -> 4, of which waited for: 4 -> 4; matrix products, arithmetic and copies ran while one was open for 2% -> 4% of each run, Pallas kernels for 0% -> 0%
where the time goes in v1:
time: 253 us; the launch traced here: 252 us
  waiting for transfers between devices  174 us (69%)
  matrix products  25.2 us (10%)
  blocking collectives  17.7 us (7%)
  between operations  13.5 us (5%)
  starting transfers between devices  9.31 us (4%)
  local copies, waits for them, and re-layouts  8.88 us (4%)
  other arithmetic  3.73 us (1%)
    all_gather x1, waiting for transfers between devices, shards(): lax.all_gather(w_down, 'dp', axis=1, tiled=True)  80.2 us
    all_to_all x1, waiting for transfers between devices, shards(): lax.all_to_all(jnp.stack([out_grads] * lax.axis_size('tensor')), 'tensor'...  55.9 us
    all_gather x1, waiting for transfers between devices, shards(): lax.all_gather(jnp.concatenate([in_high, in_low], axis=1), 'tensor', axis=0)  31.2 us
    dot_general x1, matrix products, shards(): out_part = jnp.dot(up_grad, proj_out, preferred_element_type=jnp.float32)  22.1 us
    all_to_all x1, blocking collectives, place(): got = lax.all_to_all(spread, 'dp', split_axis=0, concat_axis=0, tiled=True)  17.7 us
    all_to_all x1, waiting for transfers between devices, shards(): lax.all_to_all(part, 'tensor', split_axis=0, concat_axis=0, tiled=True)  6.05 us
  transfers between devices with their start and end apart: 4, of which 4 were waited for; matrix products, arithmetic and copies ran while one was open for 4% of the time, Pallas kernels for 0%

profile of v1, /device:TPU:32, one launch (start us, length us, event | category | flops | bytes accessed | tf_op | source)
XLA Modules:
  0.0 252.4 jit_solution(1593732881167011636)
XLA Ops:
  6.5 0.0 copy-start
  6.5 0.0 all-gather.6.cloned.1.call-start
  6.5 1.2 copy-done
  7.7 1.3 subtract_convert_fusion
  9.0 0.7 pad_maximum_fusion
  9.7 0.0 all-gather.6.cloned.1.call-update
  9.7 0.0 all-gather.4.cloned.1.call-start
  9.8 0.7 all-gather.4.cloned.1.call-update
  10.5 1.5 copy.12
  12.0 3.9 %stack.2 = bf16[8,896,512]{1,2,0:T(8,128)(2,1)} broadcast(bf16[896,512]{0,1:T(8,128)(2,1)S(1)} %copy.12), dimensions={1,2} | broadcast | bytes 8257536 | tf_op jit(solution)/shard_map/stack | solution.py:37
  15.9 5.0 %all-to-all-start = ((bf16[8,896,512]{1,2,0:T(8,128)(2,1)}), bf16[8,896,512]{1,2,0:T(8,128)(2,1)}, u32[]{:S(2)}, u32[]{:S(2)}) async-start(bf16[8,896,512]{1,2,0:T(8,128)(2,1)} %stack.2), calls=%async_computation | async-start | bytes 14680064 | tf_op jit(solution)/shard_map/all_to_all | solution.py:37
  20.9 0.0 copy-done.3
  20.9 0.1 select_reduce_fusion
  21.1 0.1 fusion.9
  21.1 31.2 %all-gather.6.cloned.1.call-done = bf16[7168,128]{0,1:T(8,128)(2,1)} async-done(((bf16[896,128]{0,1:T(8,128)(2,1)}), bf16[7168,128]{0,1:T(8,128)(2,1)}) %all-gather.6.cloned.1.call-update) | async-done | bytes 1835024 | tf_op jit(solution)/shard_map/all_gather | solution.py:39
  52.3 1.9 convert_element_type.46
  54.2 0.0 copy-start.1
  54.2 0.6 copy.14
  54.9 0.9 bitcast_reduce_fusion
  55.8 55.9 %all-to-all-done = bf16[8,896,512]{1,2,0:T(8,128)(2,1)} async-done(((bf16[8,896,512]{1,2,0:T(8,128)(2,1)}), bf16[8,896,512]{1,2,0:T(8,128)(2,1)}, u32[]{:S(2)}, u32[]{:S(2)}) %all-to-all-start) | async-done | bytes 7340064 | tf_op jit(solution)/shard_map/all_to_all | solution.py:37
  111.7 80.2 %all-gather.4.cloned.1.call-done = bf16[1792,4096]{1,0:T(8,128)(2,1)} async-done(((bf16[1792,128]{1,0:T(8,128)(2,1)}), bf16[1792,4096]{1,0:T(8,128)(2,1)}) %all-gather.4.cloned.1.call-update) | async-done | bytes 14680080 | tf_op jit(solution)/shard_map/all_gather | solution.py:45
  191.9 0.0 copy-done.1
  191.9 22.1 %fusion.4 = f32[896,64,1]{0,1,2:T(8,128)S(1)} fusion(bf16[1792,64]{0,1:T(8,128)(2,1)S(1)} %copy-done.1, bf16[896,1792]{1,0:T(8,128)(2,1)} %param.10, bf16[896,4096]{0,1:T(8,128)(2,1)} %bitcast.2, bf16[1792,4096]{1,0:T(8,128)(2,1)} %all-gather.4.cloned.1.call-done), kind=kOutput, calls=%fused_computation.7 | convolution fusion | flops 13363675136 | bytes 25690112 | tf_op jit(solution)/shard_map/dot_general | solution.py:50
  214.0 1.7 fusion.1
  215.7 0.1 reshape.95
  215.8 0.7 copy.16
  216.5 4.3 %all-to-all-start.1 = ((f32[8,8,512]{2,1,0:T(8,128)}), f32[8,8,512]{2,1,0:T(8,128)S(1)}, u32[]{:S(2)}, u32[]{:S(2)}) async-start(f32[8,8,512]{2,1,0:T(8,128)} %bitcast.24), calls=%async_computation.1 | async-start | bytes 262144 | tf_op jit(solution)/shard_map/all_to_all | solution.py:54
  220.8 0.1 dynamic_slice.3
  220.9 6.1 %all-to-all-done.1 = f32[8,8,512]{2,1,0:T(8,128)S(1)} async-done(((f32[8,8,512]{2,1,0:T(8,128)}), f32[8,8,512]{2,1,0:T(8,128)S(1)}, u32[]{:S(2)}, u32[]{:S(2)}) %all-to-all-start.1) | async-done | bytes 131104 | tf_op jit(solution)/shard_map/all_to_all | solution.py:54
  226.9 0.2 fusion.3
  227.2 17.7 %all_to_all.19 = bf16[32,8,512]{2,1,0:T(8,128)(2,1)S(1)} all-to-all(bf16[32,8,512]{2,1,0:T(8,128)(2,1)S(1)} %fusion.3), channel_id=1, replica_groups=mesh['dp'=32,'tensor'=8] {'dp'}, dimensions={0} | all-to-all | bytes 524288 | tf_op jit(solution)/shard_map/all_to_all | solution.py:23
  244.9 0.7 reshape.96
  (8 shorter events, 0.1 us)
Async XLA Ops:
  6.5 1.2 copy-start
  6.5 45.8 %all-gather.6.cloned.1.call-start = ((), (), s32[]{:S(2)}) async-start(), calls=%async_computation.4 | async-start | bytes 2064384 | tf_op jit(solution)/shard_map/all_gather | solution.py:39
  9.7 182.2 %all-gather.4.cloned.1.call-start = ((), (), s32[]{:S(2)}) async-start(), calls=%async_computation.3 | async-start | bytes 15138816 | tf_op jit(solution)/shard_map/all_gather | solution.py:45
  15.9 5.0 %copy-start.3 = (s32[1,8]{1,0:T(1,128)S(1)}, s32[1,8]{1,0:T(1,128)}, u32[]{:S(2)}) copy-start(s32[1,8]{1,0:T(1,128)} %param.14) | copy-start | bytes 100
  15.9 95.7 %all-to-all-start = ((bf16[8,896,512]{1,2,0:T(8,128)(2,1)}), bf16[8,896,512]{1,2,0:T(8,128)(2,1)}, u32[]{:S(2)}, u32[]{:S(2)}) async-start(bf16[8,896,512]{1,2,0:T(8,128)(2,1)} %stack.2), calls=%async_computation | async-start | bytes 14680064 | tf_op jit(solution)/shard_map/all_to_all | solution.py:37
  54.2 137.7 %copy-start.1 = (bf16[1792,64]{0,1:T(8,128)(2,1)S(1)}, bf16[1792,64]{0,1:T(8,128)(2,1)}, u32[]{:S(2)}) copy-start(bf16[1792,64]{0,1:T(8,128)(2,1)} %param.13) | copy-start | bytes 688132
  191.9 28.9 %copy-start.2 = (s32[256]{0:T(256)S(1)}, s32[256]{0:T(256)}, u32[]{:S(2)}) copy-start(s32[256]{0:T(256)} %param.15) | copy-start | bytes 3076
  216.5 10.4 %all-to-all-start.1 = ((f32[8,8,512]{2,1,0:T(8,128)}), f32[8,8,512]{2,1,0:T(8,128)S(1)}, u32[]{:S(2)}, u32[]{:S(2)}) async-start(f32[8,8,512]{2,1,0:T(8,128)} %bitcast.24), calls=%async_computation.1 | async-start | bytes 262144 | tf_op jit(solution)/shard_map/all_to_all | solution.py:54
Sparse Core Ops, SparseCore 0:
  9.8 42.4 all-gather.5
  54.8 137.0 all-gather.3
